TPU v7x, 32 devices: a whole 2x2x4 slice. The times are simulated.
32 devices in a mesh: dp: 16 (over z, y, core), tensor: 2 (over x).
Axes of the slice: x: 2, y: 2, z: 4, core: 2. Of those that a mesh axis runs over, the one named last changes fastest.
Arguments:
- hidden: bfloat16 [8192, 768], P('dp'), may hold values from -6 to 6
- spatial: bfloat16 [8192, 768], P('dp'), may hold values from -6 to 6
- visual: bfloat16 [8192, 768], P('dp'), may hold values from -6 to 6
- vis_len: int32 [16], P('dp'), may hold values from 256 to 512, as said below
- text_box: int32 [8192], P('dp'), may hold values from 0 to 63
- vis_box: int32 [8192], P('dp'), may hold values from 0 to 63
- text_weight_matrix: bfloat16 [5, 768, 768], P(None, None, 'tensor'), may hold values from -0.21875 to 0.21875
- w_vis: bfloat16 [3, 768, 768], P(None, None, 'tensor'), may hold values from -0.21875 to 0.21875
- w_out: bfloat16 [2, 768, 768], P(None, 'tensor'), may hold values from -0.875 to 0.875
- rel_table: float32 [12, 256], P('tensor'), may hold values from -3 to 3
- space_tables: float32 [2, 12, 128], P(None, 'tensor'), may hold values from -3 to 3
- norm_gain: float32 [2, 768], replicated, may hold values from 0.5 to 1.5
- norm_bias: float32 [2, 768], replicated, may hold values from -2 to 2
- w_up: bfloat16 [768, 3072], P(None, 'tensor'), may hold values from -0.21875 to 0.21875
- b_up: float32 [3072], P('tensor'), may hold values from -2 to 2
- w_down: bfloat16 [3072, 768], P('tensor'), may hold values from -0.109375 to 0.109375
- b_down: float32 [768], replicated, may hold values from -2 to 2
- cotangent: bfloat16 [8192, 768], P('dp'), may hold values from -6 to 6
Outputs:
- result: bfloat16 [8192, 768], P('dp')
- g_hidden: bfloat16 [8192, 768], P('dp')
- g_spatial: float32 [8192, 768], P('dp')
- g_visual: float32 [8192, 768], P('dp')
- g_w_text: float32 [5, 768, 768], P(None, 'dp', 'tensor')
- g_w_vis: float32 [3, 768, 768], P(None, 'dp', 'tensor')
- g_w_out: float32 [2, 768, 768], P(None, 'tensor', 'dp')
- g_rel_table: float32 [12, 256], P('tensor')
- g_space_tables: float32 [2, 12, 128], P(None, 'tensor')
- g_norm_gain: float32 [2, 768], replicated
- g_norm_bias: float32 [2, 768], replicated
- g_w_up: float32 [768, 3072], P('dp', 'tensor')
- g_b_up: float32 [3072], P('tensor')
- g_w_down: float32 [3072, 768], P('tensor', 'dp')
- g_b_down: float32 [768], replicated
Inputs may be any that keep to these rules, and one draw needn't show every extreme that they name: `vis_len`: each page has 256 or 512 visual tokens.
All inputs are finite; a program needn't handle non-finite values.
Results may differ from a plain program's by a relative error of at most 0.014.
The roundings to bfloat16 on the way count: a program that leaves them out, or rounds other values in their place, can miss the bound.
Values sent between devices are 32-bit elements; how exact they have to be, the bound alone decides.
No kernel may reach another device: no remote copies, remote signals or barrier semaphores. Data moves between devices by JAX's collectives and lax.ppermute only.
A program may use at most 320 MiB of HBM per device.

v0:
```python
from functools import partial

import jax
import jax.numpy as jnp
from jax import lax
from jax.sharding import PartitionSpec as P

HD = 64
TEXT = 512
VSLOT = 512
NREL = 256
NBOX = 64


EPSILON = 1e-05
MASKED = -1e30


def layer_norm(values, scales, shifts):
    centred = values - jnp.mean(values, -1, keepdims=True)
    variance = jnp.mean(centred * centred, -1, keepdims=True)
    return centred * lax.rsqrt(variance + EPSILON) * scales + shifts


def reshape_into_heads(values):
    return values.reshape(values.shape[0], -1, HD).transpose(1, 0, 2)


def from_heads(values):
    return values.transpose(1, 0, 2).reshape(values.shape[1], -1)


def mixed_product(pattern, left_side, right_side):
    return jnp.einsum(pattern, left_side, right_side, preferred_element_type=jnp.float32)


def box_bias(space_table, row_indicator, column_indicator):
    buckets = (
        lax.broadcasted_iota(jnp.int32, (NBOX, NBOX), 0)
        - lax.broadcasted_iota(jnp.int32, (NBOX, NBOX), 1)
        + NBOX
    )
    pairwise_lookup = jnp.take(space_table, buckets, axis=1)
    leading_portion = jnp.einsum(
        "ez,tzr->ter", row_indicator, pairwise_lookup, precision=lax.Precision.HIGHEST
    )
    return jnp.einsum(
        "rfz,pz->rfp", leading_portion, column_indicator, precision=lax.Precision.HIGHEST
    )


def text_bias(rel_table, space_table, rel_index, text_onehot):
    return jnp.take(rel_table, rel_index, axis=1) + box_bias(space_table, text_onehot, text_onehot)


def image_bias(space_table, text_onehot, vis_onehot):
    return box_bias(space_table, text_onehot, vis_onehot)


def log_total(scores):
    row_peak = jnp.max(scores, -1, keepdims=True)
    return row_peak + jnp.log(jnp.sum(jnp.exp(scores - row_peak), -1, keepdims=True))


def scores_back(probs, grad_out, values):
    grad_probs = mixed_product("hqd,hkd->hqk", grad_out, values)
    inner_sum = jnp.sum(grad_probs * probs, -1, keepdims=True)
    return (probs * (grad_probs - inner_sum)).astype(jnp.bfloat16)


def page_pass(weights, rel_index, page_items):
    (
        text_weight_matrix,
        w_vis,
        w_out,
        rel_table,
        space_tables,
        norm_gain,
        norm_bias,
        w_up,
        b_up,
        w_down,
        b_down,
    ) = weights
    hidden, spatial, visual, length, text_box, vis_box, cotangent = page_items
    scale = HD ** (-0.5)
    text_proj = mixed_product("sd,pde->pse", hidden, text_weight_matrix[:3]).astype(jnp.bfloat16)
    space_proj = mixed_product("sd,pde->pse", spatial, text_weight_matrix[3:]).astype(jnp.bfloat16)
    image_query = mixed_product("sd,de->se", hidden, w_vis[0]).astype(jnp.bfloat16)
    image_proj = mixed_product("sd,pde->pse", visual, w_vis[1:]).astype(jnp.bfloat16)
    text_query, text_key_rows, text_values = (
        reshape_into_heads(text_proj[0]),
        reshape_into_heads(text_proj[1]),
        reshape_into_heads(text_proj[2]),
    )
    space_query, space_keys = (reshape_into_heads(space_proj[0]), reshape_into_heads(space_proj[1]))
    image_heads = reshape_into_heads(image_query)
    image_keys, image_values = (
        reshape_into_heads(image_proj[0]),
        reshape_into_heads(image_proj[1]),
    )
    box_range = lax.broadcasted_iota(jnp.int32, (1, NBOX), 1)
    text_onehot = (text_box[:, None] == box_range).astype(jnp.float32)
    vis_onehot = (vis_box[:, None] == box_range).astype(jnp.float32)
    valid_keys = lax.broadcasted_iota(jnp.int32, (1, 1, vis_box.shape[0]), 2) < length
    text_biases, text_bias_back = jax.vjp(
        partial(text_bias, rel_index=rel_index, text_onehot=text_onehot), rel_table, space_tables[0]
    )
    image_biases, image_bias_back = jax.vjp(
        partial(image_bias, text_onehot=text_onehot, vis_onehot=vis_onehot), space_tables[1]
    )
    text_raw = mixed_product("hqd,hkd->hqk", text_query, text_key_rows) + mixed_product(
        "hqd,hkd->hqk", space_query, space_keys
    )
    text_scores = text_raw * scale + text_biases
    image_raw = mixed_product("hqd,hkd->hqk", image_heads, image_keys) * scale + image_biases
    image_scores = jnp.where(valid_keys, image_raw, MASKED)
    text_probs = jnp.exp(text_scores - log_total(text_scores))
    image_probs = jnp.exp(image_scores - log_total(image_scores))
    text_low = text_probs.astype(jnp.bfloat16)
    image_low = image_probs.astype(jnp.bfloat16)
    text_out = mixed_product("hqk,hkd->hqd", text_low, text_values).astype(jnp.bfloat16)
    image_out = mixed_product("hqk,hkd->hqd", image_low, image_values).astype(jnp.bfloat16)
    merged = jnp.concatenate([from_heads(text_out), from_heads(image_out)], 1)
    out_flat = w_out.reshape(-1, w_out.shape[2])
    attention = lax.psum(mixed_product("se,ed->sd", merged, out_flat), "tensor")
    normed, norm_one_back = jax.vjp(
        layer_norm, hidden.astype(jnp.float32) + attention, norm_gain[0], norm_bias[0]
    )
    normed_low = normed.astype(jnp.bfloat16)
    pre_gelu = mixed_product("sd,df->sf", normed_low, w_up) + b_up
    activated, gelu_back = jax.vjp(partial(jax.nn.gelu, approximate=False), pre_gelu)
    active_low = activated.astype(jnp.bfloat16)
    feed_out = lax.psum(mixed_product("sf,fd->sd", active_low, w_down), "tensor") + b_down
    outcome, norm_two_back = jax.vjp(layer_norm, normed + feed_out, norm_gain[1], norm_bias[1])
    grad_two, gain_two, shift_two = norm_two_back(cotangent.astype(jnp.float32))
    grad_feed = grad_two.astype(jnp.bfloat16)
    grad_b_down = jnp.sum(grad_feed.astype(jnp.float32), 0)
    grad_w_down = mixed_product("sf,sd->fd", active_low, grad_feed)
    grad_active = mixed_product("sd,fd->sf", grad_feed, w_down)
    grad_pre = gelu_back(grad_active)[0].astype(jnp.bfloat16)
    grad_b_up = jnp.sum(grad_pre.astype(jnp.float32), 0)
    grad_w_up = mixed_product("sd,sf->df", normed_low, grad_pre)
    grad_normed = grad_two + lax.psum(mixed_product("sf,df->sd", grad_pre, w_up), "tensor")
    grad_one, gain_one, shift_one = norm_one_back(grad_normed)
    grad_attention = grad_one.astype(jnp.bfloat16)
    grad_w_out = mixed_product("se,sd->ed", merged, grad_attention).reshape(w_out.shape)
    grad_merged = mixed_product("sd,ed->se", grad_attention, out_flat).astype(jnp.bfloat16)
    local_width = text_proj.shape[2]
    grad_text_out = reshape_into_heads(grad_merged[:, :local_width])
    grad_image_out = reshape_into_heads(grad_merged[:, local_width:])
    grad_text_scores = scores_back(text_probs, grad_text_out, text_values)
    grad_image_scores = scores_back(image_probs, grad_image_out, image_values)
    grad_rel, grad_space_text = text_bias_back(grad_text_scores.astype(jnp.float32))
    grad_space_image = image_bias_back(grad_image_scores.astype(jnp.float32))[0]
    grad_text_query = from_heads(
        (mixed_product("hqk,hkd->hqd", grad_text_scores, text_key_rows) * scale).astype(
            jnp.bfloat16
        )
    )
    grad_text_keys = from_heads(
        (mixed_product("hqk,hqd->hkd", grad_text_scores, text_query) * scale).astype(jnp.bfloat16)
    )
    grad_space_query = from_heads(
        (mixed_product("hqk,hkd->hqd", grad_text_scores, space_keys) * scale).astype(jnp.bfloat16)
    )
    grad_space_keys = from_heads(
        (mixed_product("hqk,hqd->hkd", grad_text_scores, space_query) * scale).astype(jnp.bfloat16)
    )
    grad_text_values = from_heads(
        mixed_product("hqk,hqd->hkd", text_low, grad_text_out).astype(jnp.bfloat16)
    )
    grad_image_query = from_heads(
        (mixed_product("hqk,hkd->hqd", grad_image_scores, image_keys) * scale).astype(jnp.bfloat16)
    )
    grad_image_keys = from_heads(
        (mixed_product("hqk,hqd->hkd", grad_image_scores, image_heads) * scale).astype(jnp.bfloat16)
    )
    grad_image_values = from_heads(
        mixed_product("hqk,hqd->hkd", image_low, grad_image_out).astype(jnp.bfloat16)
    )
    text_stack = jnp.stack([grad_text_query, grad_text_keys, grad_text_values])
    space_stack = jnp.stack([grad_space_query, grad_space_keys])
    image_stack = jnp.stack([grad_image_keys, grad_image_values])
    grad_w_text = jnp.concatenate(
        [
            mixed_product("sd,pse->pde", hidden, text_stack),
            mixed_product("sd,pse->pde", spatial, space_stack),
        ],
        0,
    )
    grad_w_image = jnp.concatenate(
        [
            mixed_product("sd,se->de", hidden, grad_image_query)[None],
            mixed_product("sd,pse->pde", visual, image_stack),
        ],
        0,
    )
    hidden_part = mixed_product("pse,pde->sd", text_stack, text_weight_matrix[:3]) + mixed_product(
        "se,de->sd", grad_image_query, w_vis[0]
    )
    spatial_portion = mixed_product("pse,pde->sd", space_stack, text_weight_matrix[3:])
    visual_part = mixed_product("pse,pde->sd", image_stack, w_vis[1:])
    grad_hidden, grad_spatial, grad_visual = lax.psum(
        (hidden_part, spatial_portion, visual_part), "tensor"
    )
    grad_hidden = grad_hidden + grad_one
    page_outputs = (
        outcome.astype(jnp.bfloat16),
        grad_hidden.astype(jnp.bfloat16),
        grad_spatial,
        grad_visual,
    )
    large_grads = (grad_w_text, grad_w_image, grad_w_out, grad_w_up, grad_w_down)
    small_grads = (
        grad_rel,
        jnp.stack([grad_space_text, grad_space_image]),
        jnp.stack([gain_one, gain_two]),
        jnp.stack([shift_one, shift_two]),
        grad_b_up,
        grad_b_down,
    )
    return (page_outputs, large_grads, small_grads)


def on_device(
    hidden,
    spatial,
    visual,
    vis_len,
    text_box,
    vis_box,
    text_weight_matrix,
    w_vis,
    w_out,
    rel_table,
    space_tables,
    norm_gain,
    norm_bias,
    w_up,
    b_up,
    w_down,
    b_down,
    cotangent,
):
    weights = (
        text_weight_matrix,
        w_vis,
        w_out,
        rel_table,
        space_tables,
        norm_gain,
        norm_bias,
        w_up,
        b_up,
        w_down,
        b_down,
    )
    page_count = hidden.shape[0] // TEXT
    width = hidden.shape[1]
    position = lax.broadcasted_iota(jnp.int32, (TEXT,), 0)
    rel_index = (
        jnp.clip(position[None, :] - position[:, None], -(NREL // 2), NREL // 2 - 1) + NREL // 2
    )
    page_inputs = (
        hidden.reshape(page_count, TEXT, width),
        spatial.reshape(page_count, TEXT, width),
        visual.reshape(page_count, VSLOT, width),
        vis_len,
        text_box.reshape(page_count, TEXT),
        vis_box.reshape(page_count, VSLOT),
        cotangent.reshape(page_count, TEXT, width),
    )
    local_large = (text_weight_matrix, w_vis, w_out, w_up, w_down)
    small_zero = tuple(
        (
            jnp.zeros(member.shape, jnp.float32)
            for member in (rel_table, space_tables, norm_gain, norm_bias, b_up, b_down)
        )
    )
    large_zero = tuple((jnp.zeros(member.shape, jnp.float32) for member in local_large))

    def page_step(totals, page_slice):
        page_outputs, large_grads, small_grads = page_pass(weights, rel_index, page_slice)
        totals = jax.tree.map(jnp.add, totals, (large_grads, small_grads))
        return (totals, page_outputs)

    (large_total, small_total), page_results = lax.scan(
        page_step, (large_zero, small_zero), page_inputs
    )
    large_final = (
        lax.psum_scatter(large_total[0], "dp", scatter_dimension=1, tiled=True),
        lax.psum_scatter(large_total[1], "dp", scatter_dimension=1, tiled=True),
        lax.psum_scatter(large_total[2], "dp", scatter_dimension=2, tiled=True),
        lax.psum_scatter(large_total[3], "dp", scatter_dimension=0, tiled=True),
        lax.psum_scatter(large_total[4], "dp", scatter_dimension=1, tiled=True),
    )
    small_final = lax.psum(small_total, "dp")
    return (
        page_results[0].reshape(-1, width),
        page_results[1].reshape(-1, width),
        page_results[2].reshape(-1, width),
        page_results[3].reshape(-1, width),
        large_final[0],
        large_final[1],
        large_final[2],
        small_final[0],
        small_final[1],
        small_final[2],
        small_final[3],
        large_final[3],
        small_final[4],
        large_final[4],
        small_final[5],
    )


def solution(mesh):
    return jax.shard_map(
        on_device,
        mesh=mesh,
        in_specs=(
            P("dp", None),
            P("dp", None),
            P("dp", None),
            P("dp"),
            P("dp"),
            P("dp"),
            P(None, None, "tensor"),
            P(None, None, "tensor"),
            P(None, "tensor", None),
            P("tensor", None),
            P(None, "tensor", None),
            P(),
            P(),
            P(None, "tensor"),
            P("tensor"),
            P("tensor", None),
            P(),
            P("dp", None),
        ),
        out_specs=(
            P("dp", None),
            P("dp", None),
            P("dp", None),
            P("dp", None),
            P(None, "dp", "tensor"),
            P(None, "dp", "tensor"),
            P(None, "tensor", "dp"),
            P("tensor", None),
            P(None, "tensor", None),
            P(),
            P(),
            P("dp", "tensor"),
            P("tensor"),
            P("tensor", "dp"),
            P(),
        ),
        check_vma=False,
    )
```

profile of v0, /device:TPU:0, one launch (start us, length us, event | category | flops | bytes accessed | tf_op | source)
XLA Modules:
  0.0 3147.0 jit_solution(5310134026573920675)
XLA Ops:
  11.9 14.2 gather_fusion.2
  26.0 3.3 copy.176
  34.6 4.0 fusion.110
  45.3 14.2 gather_fusion.1
  59.4 3.3 copy.171
  67.3 865.7 %gather_fusion = f32[262144,6]{1,0:T(8,128)} fusion(f32[6,256]{0,1:T(8,128)S(1)} %copy.166, s32[262144]{0:T(1024)S(1)} %broadcast_clamp_fusion), kind=kCustom, calls=%fused_computation.2 | custom fusion | bytes 13631488 | tf_op jit(solution)/shard_map/while/body/eval_jaxpr/jvp(jit(_take))/gather | solution.py:53
  933.0 72.5 %copy.168 = f32[512,512,6]{0,1,2:T(8,128)} copy(f32[512,512,6]{2,1,0:T(8,128)} %bitcast.12) | data formatting | bytes 12582912 | tf_op jit(solution)/shard_map/while/body/eval_jaxpr/jvp(jit(_take))/gather | solution.py:53
  1009.1 4.2 fusion.113
  1013.4 7.8 fusion.111
  1029.2 52.9 %all-reduce.9.cloned.1.call-done = f32[512,768]{1,0:T(8,128)} async-done(((f32[512,768]{1,0:T(8,128)}), f32[512,768]{1,0:T(8,128)}) %all-reduce.9.cloned.1.call-update) | async-done | bytes 1572880 | tf_op jit(solution)/shard_map/while/body/eval_jaxpr/psum | solution.py:126
  1085.1 9.6 multiply_convert_fusion.2
  1098.4 51.6 %all-reduce.11.cloned.1.call-done = f32[512,768]{1,0:T(8,128)} async-done(((f32[512,768]{1,0:T(8,128)}), f32[512,768]{1,0:T(8,128)}) %all-reduce.11.cloned.1.call-update) | async-done | bytes 1572880 | tf_op jit(solution)/shard_map/while/body/eval_jaxpr/psum | solution.py:134
  1164.7 51.3 %all-reduce.13.cloned.1.call-done = f32[512,768]{1,0:T(8,128)} async-done(((f32[512,768]{1,0:T(8,128)}), f32[512,768]{1,0:T(8,128)}) %all-reduce.13.cloned.1.call-update) | async-done | bytes 1572880 | tf_op jit(solution)/shard_map/while/body/eval_jaxpr/psum | solution.py:144
  1216.0 3.8 multiply_reduce_fusion.2
  1224.5 4.8 convolution_convert_fusion.7
  1229.3 7.5 multiply_reduce_fusion.1
  1236.8 7.2 convert_bitcast_fusion
  1247.4 4.3 multiply_reduce_fusion
  1251.7 4.6 convolution_convert_fusion.6
  1272.7 6.3 copy.202
  1279.9 3.7 fusion.22
  1291.0 3.5 convolution_bitcast_fusion.3
  1307.8 8.7 copy.200
  1317.6 3.7 fusion.50
  1321.3 3.3 copy.203
  1324.8 5.3 fusion.97
  1331.7 3.5 fusion.117
  1337.2 60.6 %copy.237 = f32[512,512,6]{2,1,0:T(8,128)} copy(f32[512,512,6]{0,1,2:T(8,128)} %get-tuple-element.211) | data formatting | bytes 12582912 | tf_op jit(solution)/shard_map/while/body/eval_jaxpr/convert_element_type | solution.py:154
  1402.8 1611.2 %scatter_custom_fusion = f32[6,256]{0,1:T(8,128)S(1)} fusion(s32[262144]{0:T(1024)} %bitcast.227, f32[262144,6]{1,0:T(8,128)} %bitcast.82, f32[]{:T(128)} %constant.162.clone.1), kind=kCustom, calls=%fused_computation.144 | custom fusion | flops 1572864 | bytes 6656 | tf_op jit(solution)/shard_map/while/body/eval_jaxpr/transpose(jvp(jit(_take)))/scatter-add | solution.py:53
  3014.0 22.4 scatter_custom_fusion.2
  3042.5 22.7 scatter_custom_fusion.1
  3065.3 62.7 %all-reduce.1 = (f32[6,256]{0,1:T(8,128)S(1)}, f32[2,6,128]{2,0,1:T(2,128)}, f32[2,768]{1,0:T(2,128)}, f32[2,768]{1,0:T(2,128)}, f32[1536]{0:T(1024)}, /*index=5*/f32[768]{0:T(1024)}) all-reduce(f32[6,256]{0,1:T(8,128)S(1)} %scatter_custom_fusion, ...), channel_id=1, replica_groups=mesh['dp'=16,'tensor'=2] {'dp'}, use_global_device_ids=true, to_apply=%region_24.26 | all-reduce | flops 8448 | bytes 67584 | tf_op jit(solution)/shard_map/psum | solution.py:298
  (333 shorter events, 126.1 us)
Async XLA Ops:
  7.2 1077.9 %copy-start = (bf16[768,1536]{1,0:T(8,128)(2,1)S(1)}, bf16[768,1536]{1,0:T(8,128)(2,1)}, u32[]{:S(2)}) copy-start(bf16[768,1536]{1,0:T(8,128)(2,1)} %param.33) | copy-start | bytes 7077892
  7.2 1074.9 %all-reduce.9.cloned.1.call-start = ((), (), s32[]{:S(2)}) async-start(), calls=%async_computation.4 | async-start | bytes 3145728 | tf_op jit(solution)/shard_map/while/body/eval_jaxpr/psum | solution.py:126
  1009.1 13.0 slice-start
  1013.4 8.8 slice-start.1
  1027.7 122.3 %all-reduce.11.cloned.1.call-start = ((), (), s32[]{:S(2)}) async-start(), calls=%async_computation.5 | async-start | bytes 3145728 | tf_op jit(solution)/shard_map/while/body/eval_jaxpr/psum | solution.py:134
  1083.9 10.7 copy-start.6
  1084.0 10.7 copy-start.58
  1084.3 10.4 copy-start.62
  1085.1 10.7 copy-start.84
  1098.3 117.7 %all-reduce.13.cloned.1.call-start = ((), (), s32[]{:S(2)}) async-start(), calls=%async_computation.6 | async-start | bytes 3145728 | tf_op jit(solution)/shard_map/while/body/eval_jaxpr/psum | solution.py:144
  1164.4 55.5 %copy-start.68 = (f32[512]{0:T(512)S(1)}, f32[512]{0:T(512)}, u32[]{:S(2)}) copy-start(f32[512]{0:T(512)} %copy-done.67) | copy-start | bytes 6148
  1164.4 55.5 %copy-start.7 = (f32[512,768]{1,0:T(8,128)S(1)}, f32[512,768]{1,0:T(8,128)}, u32[]{:S(2)}) copy-start(f32[512,768]{1,0:T(8,128)} %copy-done.6) | copy-start | bytes 4718596
  1164.4 55.5 %copy-start.56 = (f32[768]{0:T(1024)S(1)}, f32[768]{0:T(1024)}, u32[]{:S(2)}) copy-start(f32[768]{0:T(1024)} %get-tuple-element.245) | copy-start | bytes 9220
  1164.4 55.5 %copy-start.59 = (f32[512]{0:T(512)S(1)}, f32[512]{0:T(512)}, u32[]{:S(2)}) copy-start(f32[512]{0:T(512)} %copy-done.58) | copy-start | bytes 6148
  1164.4 55.5 %copy-start.63 = (f32[512]{0:T(512)S(1)}, f32[512]{0:T(512)}, u32[]{:S(2)}) copy-start(f32[512]{0:T(512)} %copy-done.62) | copy-start | bytes 6148
  1164.4 1964.3 %all-reduce.15.cloned.1.call-start = ((), (), s32[]{:S(2)}) async-start(), calls=%async_computation.11 | async-start | bytes 9437184
  1224.5 12.3 slice-start.4
  1229.3 7.5 slice-start.5
  1247.3 9.0 slice-start.2
  1247.4 9.0 slice-start.3
  1259.5 8.7 copy-start.24
  1279.0 1851.5 %all-reduce.17.cloned.1.call-start = ((), (), s32[]{:S(2)}) async-start(), calls=%async_computation.12 | async-start | bytes 9437184 | tf_op jit(solution)/shard_map/while/body/eval_jaxpr/psum | solution.py:204
  1300.7 1832.2 %reduce-scatter.5.cloned.1.call-start = ((), (), s32[]{:S(2)}) async-start(), calls=%async_computation.7 | async-start | bytes 10027008 | tf_op jit(solution)/shard_map/reduce_scatter | solution.py:292
  1316.5 1818.3 %reduce-scatter.7.cloned.1.call-start = ((), (), s32[]{:S(2)}) async-start(), calls=%async_computation.8 | async-start | bytes 2506752 | tf_op jit(solution)/shard_map/reduce_scatter | solution.py:294
  1324.7 1810.1 %reduce-scatter.9.cloned.1.call-start = ((), (), s32[]{:S(2)}) async-start(), calls=%async_computation.9 | async-start | bytes 5013504 | tf_op jit(solution)/shard_map/reduce_scatter | solution.py:295
  1330.1 1804.8 %reduce-scatter.11.cloned.1.call-start = ((), (), s32[]{:S(2)}) async-start(), calls=%async_computation.10 | async-start | bytes 5013504 | tf_op jit(solution)/shard_map/reduce_scatter | solution.py:296
  1337.2 60.6 %copy-start.79 = (s32[512]{0:T(512)S(1)}, s32[512]{0:T(512)}, u32[]{:S(2)}) copy-start(s32[512]{0:T(512)} %param.25) | copy-start | bytes 6148
  3036.4 28.8 copy-start.77
  3036.4 28.8 copy-start.76
  3036.4 28.9 copy-start.70
  3036.4 28.9 copy-start.80
  3039.1 91.4 %copy-start.9 = (f32[512,768]{1,0:T(8,128)S(1)}, f32[512,768]{1,0:T(8,128)}, u32[]{:S(2)}) copy-start(f32[512,768]{1,0:T(8,128)} %copy-done.8) | copy-start | bytes 4718596
  (78 other events, 221.6 us)
Sparse Core Ops, SparseCore 0:
  1027.8 54.1 all-reduce.8
  1098.5 51.4 all-reduce.10
  1164.5 51.4 all-reduce.12
  1279.1 116.9 all-reduce.14
  1399.3 119.5 all-reduce.16
  1522.9 111.3 reduce-scatter.4
  1639.2 62.7 reduce-scatter.6
  1706.4 74.5 reduce-scatter.8
  1786.0 74.5 reduce-scatter.10
where the time goes:
time: 3160 us; the launch traced here: 3150 us
  other arithmetic  1690 us (53%)
  local copies, waits for them, and re-layouts  1100 us (35%)
  waiting for transfers between devices  156 us (5%)
  matrix products  120 us (4%)
  blocking collectives  62.7 us (2%)
    scatter-add x1, other arithmetic, text_bias(): jnp.take(rel_table, rel_index, axis=1)  1610 us
    gather x2, local copies, waits for them, and re-layouts, text_bias(): jnp.take(rel_table, rel_index, axis=1)  938 us
    dot_general x36, matrix products, mixed_product(): jnp.einsum(pattern, left_side, right_side, preferred_element_type=jnp.flo...  99.6 us
  transfers between devices with their start and end apart: 9, of which 3 were waited for; matrix products, arithmetic and copies ran while one was open for 57% of the time, Pallas kernels for 0%

commit v1 on v0

v1 whole, which is shorter than its diff:
```python
from functools import partial

import jax
import jax.numpy as jnp
from jax import lax
from jax.experimental import pallas as pl
from jax.experimental.pallas import tpu as pltpu
from jax.sharding import PartitionSpec as P

HD = 64
PAIR = 2 * HD
TEXT = 512
NREL = 256
NBOX = 64
BLK = 128
EPSILON = 1e-05
MASKED = -1e30
SCALE = HD ** (-0.5)
F32 = jnp.float32
BF16 = jnp.bfloat16
MIB = 1 << 20


def mm(a, b):
    return jnp.dot(a, b, preferred_element_type=F32)


def mm_nt(a, b):
    return lax.dot_general(a, b, (((1,), (1,)), ((), ())), preferred_element_type=F32)


def mm_tn(a, b):
    return lax.dot_general(a, b, (((0,), (0,)), ((), ())), preferred_element_type=F32)


def call(body, name, grid, args, in_specs, outs, out_specs, scratch=(), flops=0, nbytes=0):
    return pl.pallas_call(
        body,
        out_shape=outs,
        grid_spec=pltpu.PrefetchScalarGridSpec(
            num_scalar_prefetch=0,
            grid=grid,
            in_specs=in_specs,
            out_specs=out_specs,
            scratch_shapes=list(scratch),
        ),
        compiler_params=pltpu.CompilerParams(
            dimension_semantics=("arbitrary",) * len(grid), vmem_limit_bytes=44 * MIB
        ),
        cost_estimate=pl.CostEstimate(flops=int(flops), bytes_accessed=int(nbytes), transcendentals=0),
        name=name,
    )(*args)


def whole(x):
    nd = x.ndim
    return pl.BlockSpec(x.shape, lambda p: (0,) * nd)


def sds(shape, dtype=F32):
    return jax.ShapeDtypeStruct(shape, dtype)


def pair_block(rows, width):
    return pl.BlockSpec((rows, width), lambda p: (0, p))


def lead_block(x):
    nd = x.ndim
    return pl.BlockSpec((1,) + x.shape[1:], lambda p: (p,) + (0,) * (nd - 1))


def proj_body(hid, spa, vis, wt, wv, tqs, tks, tv, vq, vk, vv):
    ph = mm(hid[...], jnp.concatenate([wt[0], wt[1], wt[2], wv[0]], 1)).astype(BF16)
    ps = mm(spa[...], jnp.concatenate([wt[3], wt[4]], 1)).astype(BF16)
    pv = mm(vis[...], jnp.concatenate([wv[1], wv[2]], 1)).astype(BF16)
    scale = jnp.asarray(SCALE, BF16)
    tqs[0, :, :PAIR] = ph[:, :PAIR] * scale
    tqs[0, :, PAIR:] = ps[:, :PAIR] * scale
    tks[0, :, :PAIR] = ph[:, PAIR : 2 * PAIR]
    tks[0, :, PAIR:] = ps[:, PAIR:]
    tv[0] = ph[:, 2 * PAIR : 3 * PAIR]
    vq[0] = ph[:, 3 * PAIR :] * scale
    vk[0] = pv[:, :PAIR]
    vv[0] = pv[:, PAIR:]


def projections(hidden, spatial, visual, w_text, w_vis):
    n, d = hidden.shape
    pairs = w_text.shape[2] // PAIR
    wide, slim = sds((pairs, n, 2 * PAIR), BF16), sds((pairs, n, PAIR), BF16)
    outs = [wide, wide, slim, slim, slim, slim]
    return call(
        proj_body,
        "projections",
        (pairs,),
        (hidden, spatial, visual, w_text, w_vis),
        [
            whole(hidden),
            whole(spatial),
            whole(visual),
            pl.BlockSpec((5, d, PAIR), lambda p: (0, 0, p)),
            pl.BlockSpec((3, d, PAIR), lambda p: (0, 0, p)),
        ],
        outs,
        [lead_block(o) for o in outs],
        flops=2 * n * d * 8 * pairs * PAIR,
        nbytes=9e6,
    )


def head_mask(h, width):
    lane = lax.broadcasted_iota(jnp.int32, (1, width), 1)
    return jnp.where((lane // HD) % 2 == h, 1.0, 0.0).astype(BF16)


def one_hot(box):
    lane = lax.broadcasted_iota(jnp.int32, (box.shape[0], PAIR), 1)
    return jnp.where(lane % HD == box, 1.0, 0.0).astype(BF16)


def box_rows(reversed_row):
    wide = jnp.broadcast_to(reversed_row, (NBOX, PAIR))
    rolled = pltpu.roll(wide, NBOX + 1, 1, stride=1, stride_axis=0)
    high = rolled.astype(BF16).astype(F32)
    rest = pltpu.roll(rolled - high, NBOX, 1)
    lane = lax.broadcasted_iota(jnp.int32, (NBOX, PAIR), 1)
    both = jnp.where(lane < NBOX, high, rest)
    return jnp.concatenate([both, jnp.zeros_like(both)], 0).astype(BF16)


def rel_band(extended_row):
    wide = jnp.broadcast_to(extended_row, (BLK, 4 * BLK))
    return pltpu.roll(wide, 0, 1, stride=1, stride_axis=0)[:, BLK:]


def rel_bias(band, ends, block, blocks):
    pieces = []
    for other in range(blocks):
        step = other - block
        if step >= 2:
            pieces.append(jnp.broadcast_to(ends[1], (BLK, BLK)))
        elif step <= -2:
            pieces.append(jnp.broadcast_to(ends[0], (BLK, BLK)))
        else:
            pieces.append(band[:, (step + 1) * BLK : (step + 2) * BLK])
    return jnp.concatenate(pieces, 1)


def rel_parts(rel, h):
    row = rel[0, h : h + 1, :]
    return rel_band(row), (row[:, :1], row[:, 4 * BLK - 1 :])


def attend(scores, values):
    peak = jnp.max(scores, 1, keepdims=True)
    powers = jnp.exp(scores - peak)
    total = jnp.sum(powers, 1, keepdims=True)
    probs = (powers * (1.0 / total)).astype(BF16)
    return mm(probs, values), peak + jnp.log(total)


def forward_body(vlen, tqs, vq, tks, tv, vk, vv, tbq, tbk, vbk, rel, rows, wo, attn, to, vo, lse, *, first):
    count = tqs.shape[1]
    keys_n = tks.shape[1]
    hot_q, hot_t, hot_v = one_hot(tbq[...]), one_hot(tbk[...]), one_hot(vbk[...])
    keys_t = jnp.concatenate([tks[0], hot_t], 1)
    keys_v = jnp.concatenate([vk[0], hot_v], 1)
    valid = lax.broadcasted_iota(jnp.int32, (1, keys_n), 1) < vlen[0]
    lane = lax.broadcasted_iota(jnp.int32, (BLK, PAIR), 1)
    text_out, vis_out, logs = {}, {}, {}
    for h in range(2):
        look_t = mm(hot_q, box_rows(rows[0, 0, h : h + 1, :])).astype(BF16)
        look_v = mm(hot_q, box_rows(rows[0, 1, h : h + 1, :])).astype(BF16)
        query_t = jnp.concatenate([tqs[0] * head_mask(h, 2 * PAIR), look_t], 1)
        query_v = jnp.concatenate([vq[0] * head_mask(h, PAIR), look_v], 1)
        band, ends = rel_parts(rel, h)
        for b in range(count // BLK):
            part = slice(b * BLK, (b + 1) * BLK)
            bias = rel_bias(band, ends, first // BLK + b, keys_n // BLK)
            text_out[h, b], logs[0, h, b] = attend(mm_nt(query_t[part], keys_t) + bias, tv[0])
            vis_out[h, b], logs[1, h, b] = attend(
                jnp.where(valid, mm_nt(query_v[part], keys_v), MASKED), vv[0]
            )
    weights = jnp.concatenate([wo[0], wo[1]], 0)
    for b in range(count // BLK):
        part = slice(b * BLK, (b + 1) * BLK)
        out_t = jnp.where(lane < HD, text_out[0, b], text_out[1, b]).astype(BF16)
        out_v = jnp.where(lane < HD, vis_out[0, b], vis_out[1, b]).astype(BF16)
        to[part, :] = out_t
        vo[part, :] = out_v
        kept = jnp.zeros((BLK, PAIR), F32)
        for spot, (stream, h) in enumerate(((0, 0), (0, 1), (1, 0), (1, 1))):
            kept = jnp.where(lane == spot, logs[stream, h, b], kept)
        lse[0, part, :] = kept
        term = mm(jnp.concatenate([out_t, out_v], 1), weights)

        @pl.when(pl.program_id(0) == 0)
        def _():
            attn[part, :] = term

        @pl.when(pl.program_id(0) > 0)
        def _():
            attn[part, :] += term


def forward_rows(first, count, proj, boxes, vlen, rel_ext, box_rev, w_out):
    tqs, tks, tv, vq, vk, vv = proj
    tb, vb = boxes
    pairs, n, _ = tqs.shape
    d = w_out.shape[2]
    spot = first // count

    def rows_of(x):
        return pl.BlockSpec((1, count, x.shape[2]), lambda p: (p, spot, 0))

    return call(
        partial(forward_body, first=first),
        f"attention_forward_{spot}",
        (pairs,),
        (vlen, tqs, vq, tks, tv, vk, vv, tb, tb, vb, rel_ext, box_rev, w_out),
        [
            pl.BlockSpec(memory_space=pltpu.SMEM),
            rows_of(tqs),
            rows_of(vq),
            lead_block(tks),
            lead_block(tv),
            lead_block(vk),
            lead_block(vv),
            pl.BlockSpec((count, 1), lambda p: (spot, 0)),
            whole(tb),
            whole(vb),
            lead_block(rel_ext),
            lead_block(box_rev),
            pl.BlockSpec((2, PAIR, d), lambda p: (0, p, 0)),
        ],
        [
            sds((count, d)),
            sds((count, pairs * PAIR), BF16),
            sds((count, pairs * PAIR), BF16),
            sds((pairs, count, PAIR)),
        ],
        [
            pl.BlockSpec((count, d), lambda p: (0, 0)),
            pair_block(count, PAIR),
            pair_block(count, PAIR),
            pl.BlockSpec((1, count, PAIR), lambda p: (p, 0, 0)),
        ],
        flops=pairs * 2 * 10 * count * n * PAIR,
        nbytes=4e6,
    )


def scores_gradient(probs, grad_out, values):
    grad_probs = mm_nt(grad_out, values)
    inner = jnp.sum(grad_probs * probs, 1, keepdims=True)
    return (probs * (grad_probs - inner)).astype(BF16)


def box_gradient(hot_q, spread, out):
    lane = lax.broadcasted_iota(jnp.int32, (hot_q.shape[0], NBOX), 1)
    flipped = jnp.where(lane == NBOX - 1 - hot_q, 1.0, 0.0).astype(BF16)
    high = spread.astype(BF16)
    rest = (spread - high.astype(F32)).astype(BF16)
    table = mm_tn(flipped, high) + mm_tn(flipped, rest)
    lane = lax.broadcasted_iota(jnp.int32, (NBOX, PAIR), 1)
    for h in range(2):
        mine = table if h == 0 else pltpu.roll(table, NBOX, 1)
        mine = jnp.where(lane < NBOX, mine, 0.0)
        sheared = pltpu.roll(mine, 0, 1, stride=1, stride_axis=0)
        out[0, h : h + 1, :] = jnp.sum(sheared, 0, keepdims=True)


def shear_sum(band):
    width = band.shape[1]
    rows = BLK
    while rows > 8:
        rows //= 2
        band = band[:rows] + pltpu.roll(band[rows:], width - rows, 1)
    row = lax.broadcasted_iota(jnp.int32, band.shape, 0)
    for bit in (4, 2, 1):
        band = jnp.where((row // bit) % 2 == 1, pltpu.roll(band, width - bit, 1), band)
    return jnp.sum(band, 0, keepdims=True)


def visual_back_body(
    vlen, vq, vk, vv, dvo, lse, tb, vb, rows, wv, dxq, dxv, g_vis, g_box, ds_ref, pb_ref
):
    n = vq.shape[1]
    hot_q, hot_v = one_hot(tb[...]), one_hot(vb[...])
    keys = jnp.concatenate([vk[0], hot_v], 1)
    valid = lax.broadcasted_iota(jnp.int32, (1, vk.shape[1]), 1) < vlen[0]
    dq = dkt = dvt = spread = None
    for h in range(2):
        mask = head_mask(h, PAIR)
        look = mm(hot_q, box_rows(rows[0, 1, h : h + 1, :])).astype(BF16)
        mine = vq[0] * mask
        query = jnp.concatenate([mine, look], 1)
        grad = dvo[...] * mask
        for b in range(n // BLK):
            part = slice(b * BLK, (b + 1) * BLK)
            scores = jnp.where(valid, mm_nt(query[part], keys), MASKED)
            probs = jnp.exp(scores - lse[0, part, 2 + h : 3 + h])
            pb_ref[part, :] = probs.astype(BF16)
            ds_ref[part, :] = scores_gradient(probs, grad[part], vv[0])
        ds, pb = ds_ref[...], pb_ref[...]
        terms = (mm(ds, vk[0] * mask), mm_tn(mine, ds), mm_tn(grad, pb), mm(ds, hot_v * mask))
        if h == 0:
            dq, dkt, dvt, spread = terms
        else:
            dq, dkt, dvt, spread = (a + b for a, b in zip((dq, dkt, dvt, spread), terms))
    box_gradient(tb[...], spread, g_box)
    dxq[...] = (dq * SCALE).astype(BF16)
    both = jnp.concatenate([dkt.astype(BF16), dvt.astype(BF16)], 0).T
    dxv[...] = both
    term = mm_nt(both, jnp.concatenate([wv[1], wv[2]], 1))

    @pl.when(pl.program_id(0) == 0)
    def _():
        g_vis[...] = term

    @pl.when(pl.program_id(0) > 0)
    def _():
        g_vis[...] += term


def visual_back(proj, boxes, vlen, box_rev, dvo, lse, w_vis):
    vq, vk, vv = proj[3:]
    tb, vb = boxes
    pairs, n, _ = vq.shape
    d = w_vis.shape[1]
    return call(
        visual_back_body,
        "visual_attention_backward",
        (pairs,),
        (vlen, vq, vk, vv, dvo, lse, tb, vb, box_rev, w_vis),
        [
            pl.BlockSpec(memory_space=pltpu.SMEM),
            lead_block(vq),
            lead_block(vk),
            lead_block(vv),
            pair_block(n, PAIR),
            lead_block(lse),
            whole(tb),
            whole(vb),
            lead_block(box_rev),
            pl.BlockSpec((3, d, PAIR), lambda p: (0, 0, p)),
        ],
        [
            sds((n, pairs * PAIR), BF16),
            sds((n, pairs * 2 * PAIR), BF16),
            sds((n, d)),
            sds((pairs, 8, PAIR)),
        ],
        [
            pair_block(n, PAIR),
            pair_block(n, 2 * PAIR),
            pl.BlockSpec((n, d), lambda p: (0, 0)),
            pl.BlockSpec((1, 8, PAIR), lambda p: (p, 0, 0)),
        ],
        [pltpu.VMEM((n, n), BF16), pltpu.VMEM((n, n), BF16)],
        flops=pairs * 2 * 18 * n * n * PAIR,
        nbytes=5e6,
    )


def text_back_body(
    tqs, tks, tv, dto, lse, tb, rel, rows, dxq, wt, wv, dxh, dxs, g_hid, g_spa, g_box, g_rel, ds_ref, pb_ref
):
    n = tqs.shape[1]
    hot = one_hot(tb[...])
    keys = jnp.concatenate([tks[0], hot], 1)
    dq = dkt = dvt = spread = None
    for h in range(2):
        mask, wide_mask = head_mask(h, PAIR), head_mask(h, 2 * PAIR)
        look = mm(hot, box_rows(rows[0, 0, h : h + 1, :])).astype(BF16)
        mine = tqs[0] * wide_mask
        query = jnp.concatenate([mine, look], 1)
        grad = dto[...] * mask
        band, ends = rel_parts(rel, h)
        near = [None] * 3
        low = high = jnp.zeros((BLK, BLK), F32)
        for b in range(n // BLK):
            part = slice(b * BLK, (b + 1) * BLK)
            scores = mm_nt(query[part], keys) + rel_bias(band, ends, b, n // BLK)
            probs = jnp.exp(scores - lse[0, part, h : h + 1])
            pb_ref[part, :] = probs.astype(BF16)
            ds = scores_gradient(probs, grad[part], tv[0])
            ds_ref[part, :] = ds
            ds = ds.astype(F32)
            for other in range(n // BLK):
                piece = ds[:, other * BLK : (other + 1) * BLK]
                step = other - b
                if step >= 2:
                    high = high + piece
                elif step <= -2:
                    low = low + piece
                else:
                    near[step + 1] = piece if near[step + 1] is None else near[step + 1] + piece
        ds, pb = ds_ref[...], pb_ref[...]
        sums = shear_sum(jnp.concatenate(near + [jnp.zeros((BLK, BLK), F32)], 1))
        far = jnp.concatenate(
            [jnp.sum(low, 0, keepdims=True), jnp.sum(high, 0, keepdims=True)], 1
        )
        g_rel[0, 2 * h : 2 * h + 1, :] = sums
        g_rel[0, 2 * h + 1 : 2 * h + 2, : 2 * BLK] = far
        terms = (mm(ds, tks[0] * wide_mask), mm_tn(mine, ds), mm_tn(grad, pb), mm(ds, hot * mask))
        if h == 0:
            dq, dkt, dvt, spread = terms
        else:
            dq, dkt, dvt, spread = (a + b for a, b in zip((dq, dkt, dvt, spread), terms))
    box_gradient(tb[...], spread, g_box)
    dqs = (dq * SCALE).astype(BF16)
    rest = jnp.concatenate([dkt.astype(BF16), dvt.astype(BF16)], 0).T
    to_spatial = jnp.concatenate([dqs[:, PAIR:], rest[:, PAIR : 2 * PAIR]], 1)
    to_hidden = jnp.concatenate([dqs[:, :PAIR], rest[:, :PAIR], rest[:, 2 * PAIR :]], 1)
    dxs[...] = to_spatial
    dxh[...] = to_hidden
    term_s = mm_nt(to_spatial, jnp.concatenate([wt[3], wt[4]], 1))
    term_h = mm_nt(
        jnp.concatenate([to_hidden, dxq[...]], 1),
        jnp.concatenate([wt[0], wt[1], wt[2], wv[0]], 1),
    )

    @pl.when(pl.program_id(0) == 0)
    def _():
        g_spa[...] = term_s
        g_hid[...] = term_h

    @pl.when(pl.program_id(0) > 0)
    def _():
        g_spa[...] += term_s
        g_hid[...] += term_h


def text_back(proj, boxes, rel_ext, box_rev, dto, lse, dxq, w_text, w_vis):
    tqs, tks, tv = proj[:3]
    tb = boxes[0]
    pairs, n, _ = tqs.shape
    d = w_vis.shape[1]
    return call(
        text_back_body,
        "text_attention_backward",
        (pairs,),
        (tqs, tks, tv, dto, lse, tb, rel_ext, box_rev, dxq, w_text, w_vis),
        [
            lead_block(tqs),
            lead_block(tks),
            lead_block(tv),
            pair_block(n, PAIR),
            lead_block(lse),
            whole(tb),
            lead_block(rel_ext),
            lead_block(box_rev),
            pair_block(n, PAIR),
            pl.BlockSpec((5, d, PAIR), lambda p: (0, 0, p)),
            pl.BlockSpec((3, d, PAIR), lambda p: (0, 0, p)),
        ],
        [
            sds((n, pairs * 3 * PAIR), BF16),
            sds((n, pairs * 2 * PAIR), BF16),
            sds((n, d)),
            sds((n, d)),
            sds((pairs, 8, PAIR)),
            sds((pairs, 8, 4 * BLK)),
        ],
        [
            pair_block(n, 3 * PAIR),
            pair_block(n, 2 * PAIR),
            pl.BlockSpec((n, d), lambda p: (0, 0)),
            pl.BlockSpec((n, d), lambda p: (0, 0)),
            pl.BlockSpec((1, 8, PAIR), lambda p: (p, 0, 0)),
            pl.BlockSpec((1, 8, 4 * BLK), lambda p: (p, 0, 0)),
        ],
        [pltpu.VMEM((n, n), BF16), pltpu.VMEM((n, n), BF16)],
        flops=pairs * 2 * 26 * n * n * PAIR,
        nbytes=9e6,
    )


def normalise(values):
    centred = values - jnp.mean(values, 1, keepdims=True)
    rstd = lax.rsqrt(jnp.mean(centred * centred, 1, keepdims=True) + EPSILON)
    return centred * rstd, rstd


def norm_back(grad, unit, rstd, gain):
    scaled = grad * gain
    mean_one = jnp.mean(scaled, 1, keepdims=True)
    mean_two = jnp.mean(scaled * unit, 1, keepdims=True)
    return rstd * (scaled - mean_one - unit * mean_two)


def column_sum(x):
    return jnp.sum(x, 0, keepdims=True)


def up_body(hid, own, got, norms, w_up, b_up, w_down, r1, h1, h1b, z, slope, f):
    total = hid[...].astype(F32) + (own[...] + got[...])
    unit, _ = normalise(total)
    normed = unit * norms[0:1, :] + norms[2:3, :]
    low = normed.astype(BF16)
    r1[...] = total
    h1[...] = normed
    h1b[...] = low
    u = mm(low, w_up[...]) + b_up[...]
    cdf = 0.5 * (1.0 + lax.erf(u * (0.5**0.5)))
    slope[...] = cdf + u * (jnp.exp(-0.5 * u * u) * 0.3989422804014327)
    active = (u * cdf).astype(BF16)
    z[...] = active
    f[...] = mm(active, w_down[...])


def up_rows(spot, hidden, own, got, norms, w_up, b_up, w_down):
    count, d = own.shape
    ff = w_up.shape[1]
    args = (hidden, own, got, norms, w_up, b_up, w_down)
    outs = [sds((count, d)), sds((count, d)), sds((count, d), BF16), sds((count, ff), BF16)]
    outs += [sds((count, ff)), sds((count, d))]
    return call(
        up_body,
        f"feed_forward_{spot}",
        (1,),
        args,
        [pl.BlockSpec((count, d), lambda p: (spot, 0))] + [whole(x) for x in args[1:]],
        outs,
        [whole(x) for x in outs],
        flops=4 * count * d * ff,
        nbytes=9e6,
    )


def down_body(h1, own, got, cot, norms, b_down, w_down, w_up, slope, result, dr2, df, du, pd, sums, sum_up):
    total = h1[...] + ((own[...] + got[...]) + b_down[...])
    unit, rstd = normalise(total)
    result[...] = (unit * norms[1:2, :] + norms[3:4, :]).astype(BF16)
    grad = cot[...].astype(F32)
    back = norm_back(grad, unit, rstd, norms[1:2, :])
    low = back.astype(BF16)
    dr2[...] = back
    df[...] = low
    grad_u = (slope[...] * mm_nt(low, w_down[...])).astype(BF16)
    du[...] = grad_u
    pd[...] = mm_nt(grad_u, w_up[...])
    sums[0:1, :] = column_sum(grad * unit)
    sums[1:2, :] = column_sum(grad)
    sums[2:3, :] = column_sum(low.astype(F32))
    sum_up[0:1, :] = column_sum(grad_u.astype(F32))


def down_rows(spot, h1, own, got, cotangent, norms, b_down, w_down, w_up, slope):
    count, d = own.shape
    ff = w_up.shape[1]
    args = (h1, own, got, cotangent, norms, b_down, w_down, w_up, slope)
    specs = [whole(x) for x in args]
    specs[3] = pl.BlockSpec((count, d), lambda p: (spot, 0))
    outs = [sds((count, d), BF16), sds((count, d)), sds((count, d), BF16), sds((count, ff), BF16)]
    outs += [sds((count, d)), sds((8, d)), sds((8, ff))]
    return call(
        down_body,
        f"feed_forward_backward_{spot}",
        (1,),
        args,
        specs,
        outs,
        [whole(x) for x in outs],
        flops=4 * count * d * ff,
        nbytes=9e6,
    )


def first_body(dr2, own, got, r1, norms, w_out, dr1, da, dto, dvo, sums):
    grad = dr2[...] + (own[...] + got[...])
    unit, rstd = normalise(r1[...])
    back = norm_back(grad, unit, rstd, norms[0:1, :])
    low = back.astype(BF16)
    dr1[...] = back
    da[...] = low
    dto[...] = mm_nt(low, w_out[0]).astype(BF16)
    dvo[...] = mm_nt(low, w_out[1]).astype(BF16)
    sums[0:1, :] = column_sum(grad * unit)
    sums[1:2, :] = column_sum(grad)


def first_rows(spot, dr2, own, got, r1, norms, w_out):
    count, d = own.shape
    width = w_out.shape[1]
    args = (dr2, own, got, r1, norms, w_out)
    outs = [sds((count, d)), sds((count, d), BF16)]
    outs += [sds((count, width), BF16), sds((count, width), BF16), sds((8, d))]
    return call(
        first_body,
        f"first_norm_backward_{spot}",
        (1,),
        args,
        [whole(x) for x in args],
        outs,
        [whole(x) for x in outs],
        flops=4 * count * d * width,
        nbytes=4e6,
    )


def product_body(a, b, mine, other):
    half = mine.shape[0]
    out = mm(a[...], b[...])
    mine[...] = out[:half]
    other[...] = out[half:]


def weight_product(name, rows_t, cols, block):
    d, n = rows_t.shape
    width = cols.shape[1]
    return call(
        product_body,
        name,
        (width // block,),
        (rows_t, cols),
        [whole(rows_t), pair_block(n, block)],
        [sds((d // 2, width)), sds((d // 2, width))],
        [pair_block(d // 2, block), pair_block(d // 2, block)],
        flops=2 * d * n * width,
        nbytes=4 * d * width,
    )


def attention_product_body(hid, spa, dxh, dxq, dxs, mine, other):
    half = mine.shape[0]
    out = mm(hid[...], jnp.concatenate([dxh[...], dxq[...]], 1))
    cut = out.shape[1]
    mine[:, :cut] = out[:half]
    other[:, :cut] = out[half:]
    out = mm(spa[...], dxs[...])
    mine[:, cut:] = out[:half]
    other[:, cut:] = out[half:]


def attention_product(hid_t, spa_t, dxh, dxq, dxs):
    d, n = hid_t.shape
    pairs = dxq.shape[1] // PAIR
    width = 6 * PAIR
    return call(
        attention_product_body,
        "text_projection_gradients",
        (pairs,),
        (hid_t, spa_t, dxh, dxq, dxs),
        [
            whole(hid_t),
            whole(spa_t),
            pair_block(n, 3 * PAIR),
            pair_block(n, PAIR),
            pair_block(n, 2 * PAIR),
        ],
        [sds((d // 2, pairs * width)), sds((d // 2, pairs * width))],
        [pair_block(d // 2, width), pair_block(d // 2, width)],
        flops=2 * d * n * width * pairs,
        nbytes=4 * d * width * pairs,
    )


class Links:
    def __init__(self, sizes):
        self.n = sizes["dp"]
        self.tensor = sizes["tensor"]
        n = self.n
        self.core = [(d, d ^ 1) for d in range(n)]
        self.side = [(d, d ^ 2) for d in range(n)]
        self.ring = [(d, (d + 4) % n) for d in range(n)]
        self.turns = n // 4

    def order(self):
        me = lax.axis_index("dp")
        core, side, ring = me % 2, (me // 2) % 2, me // 4
        places = []
        for c in range(2):
            for s in range(2):
                for r in range(self.turns):
                    places.append(((ring + r) % self.turns) * 4 + (side ^ s) * 2 + (core ^ c))
        return jnp.stack(places)

    def relative_rows(self, x):
        d = x.shape[1]
        rows = d // self.n
        chunks = x.T.reshape(self.n, rows, x.shape[0])
        return jnp.take(chunks, self.order(), axis=0, mode="clip").reshape(d, x.shape[0])

    def across(self, x):
        return lax.ppermute(x, "tensor", [(0, 1), (1, 0)])

    def scatter(self, halves, side_first):
        mine, other = halves
        width = mine.shape[1]
        rows = mine.shape[0] // (2 * self.turns)
        shape = (2, self.turns, rows, width)
        total = mine.reshape(shape) + lax.ppermute(other, "dp", self.core).reshape(shape)
        if side_first:
            total = total[0] + lax.ppermute(total[1], "dp", self.side)
            moving = total[self.turns - 1]
            for turn in range(self.turns - 2, -1, -1):
                moving = total[turn] + lax.ppermute(moving, "dp", self.ring)
            return moving
        moving = total[:, self.turns - 1]
        for turn in range(self.turns - 2, -1, -1):
            moving = total[:, turn] + lax.ppermute(moving, "dp", self.ring)
        return moving[0] + lax.ppermute(moving[1], "dp", self.side)

    def sum_all(self, x):
        step = 1
        while step < self.n:
            x = x + lax.ppermute(x, "dp", [(d, d ^ step) for d in range(self.n)])
            step *= 2
        return x


def on_device(
    links,
    hidden,
    spatial,
    visual,
    vis_len,
    text_box,
    vis_box,
    text_weight_matrix,
    w_vis,
    w_out,
    rel_table,
    space_tables,
    norm_gain,
    norm_bias,
    w_up,
    b_up,
    w_down,
    b_down,
    cotangent,
):
    n, d = hidden.shape
    width = w_vis.shape[2]
    pairs = width // PAIR
    ff = w_up.shape[1]
    heads = rel_table.shape[0]
    boxes = (text_box.reshape(n, 1), vis_box.reshape(-1, 1))
    rel_ext = jnp.concatenate(
        [
            jnp.broadcast_to(rel_table[:, :1], (heads, NREL // 2)),
            rel_table,
            jnp.broadcast_to(rel_table[:, NREL - 1 :], (heads, NREL // 2)),
        ],
        1,
    ).reshape(pairs, 2, 2 * NREL)
    box_rev = space_tables[:, :, ::-1].reshape(2, pairs, 2, PAIR).transpose(1, 0, 2, 3)
    norms = jnp.concatenate([norm_gain, norm_bias], 0)
    b_up_row, b_down_row = b_up.reshape(1, ff), b_down.reshape(1, d)

    proj = projections(hidden, spatial, visual, text_weight_matrix, w_vis)
    count = n // 2
    spots = range(n // count)
    front = [
        forward_rows(s * count, count, proj, boxes, vis_len, rel_ext, box_rev, w_out) for s in spots
    ]
    got = [links.across(f[0]) for f in front]
    up = [
        up_rows(s, hidden, front[s][0], got[s], norms, w_up, b_up_row, w_down) for s in spots
    ]
    got = [links.across(u[5]) for u in up]
    down = [
        down_rows(s, up[s][1], up[s][5], got[s], cotangent, norms, b_down_row, w_down, w_up, up[s][4])
        for s in spots
    ]
    got = [links.across(x[4]) for x in down]
    first = [first_rows(s, down[s][1], down[s][4], got[s], up[s][0], norms, w_out) for s in spots]

    def joined(parts, axis=0):
        return jnp.concatenate(list(parts), axis)

    result = joined(x[0] for x in down)
    dr1 = joined(x[0] for x in first)
    dto = joined(x[2] for x in first)
    dvo = joined(x[3] for x in first)
    lse = joined((f[3] for f in front), 1)

    dxq, dxv, part_vis, g_box_vis = visual_back(proj, boxes, vis_len, box_rev, dvo, lse, w_vis)
    dxh, dxs, part_hid, part_spa, g_box_text, g_rel = text_back(
        proj, boxes, rel_ext, box_rev, dto, lse, dxq, text_weight_matrix, w_vis
    )
    grad_visual = part_vis + links.across(part_vis)
    grad_spatial = part_spa + links.across(part_spa)
    grad_hidden = (dr1 + (part_hid + links.across(part_hid))).astype(BF16)

    df_t = links.relative_rows(joined(x[2] for x in down))
    h1_t = links.relative_rows(joined(u[2] for u in up))
    da_t = links.relative_rows(joined(x[1] for x in first))
    vis_t = links.relative_rows(visual)
    hid_t = links.relative_rows(hidden)
    spa_t = links.relative_rows(spatial)
    merged = jnp.concatenate([joined(f[1] for f in front), joined(f[2] for f in front)], 1)
    half_down = weight_product("down_gradient", df_t, joined(u[3] for u in up), ff // 2)
    half_up = weight_product("up_gradient", h1_t, joined(x[3] for x in down), ff // 2)
    half_out = weight_product("out_gradient", da_t, merged, width)
    half_vis = weight_product("visual_projection_gradients", vis_t, dxv, width)
    half_text = attention_product(hid_t, spa_t, dxh, dxq, dxs)

    g_w_down = links.scatter(half_down, True).T
    g_w_up = links.scatter(half_up, True)
    rows = d // links.n
    g_w_out = links.scatter(half_out, False).reshape(rows, 2, width).transpose(1, 2, 0)
    from_vis = links.scatter(half_vis, False).reshape(rows, pairs, 2, PAIR)
    from_text = links.scatter(half_text, True).reshape(rows, pairs, 6, PAIR)
    from_vis = from_vis.transpose(2, 0, 1, 3).reshape(2, rows, width)
    from_text = from_text.transpose(2, 0, 1, 3).reshape(6, rows, width)
    g_w_text = jnp.concatenate([from_text[:3], from_text[4:]], 0)
    g_w_vis = jnp.concatenate([from_text[3:4], from_vis], 0)

    rel = g_rel.reshape(pairs, 4, 2, 2 * NREL)[:, :2].reshape(heads, 2, 2 * NREL)
    near, far = rel[:, 0], rel[:, 1]
    half = NREL // 2
    low = jnp.sum(near[:, 3 * half + 1 :], 1) + near[:, 0] + jnp.sum(far[:, :half], 1)
    high = jnp.sum(near[:, 2 * half - 1 : 3 * half], 1) + jnp.sum(far[:, half : 2 * half], 1)
    g_rel_table = jnp.concatenate([low[:, None], near[:, 1 : 2 * half - 1], high[:, None]], 1)
    g_space = jnp.stack([g_box_text[:, :2], g_box_vis[:, :2]]).reshape(2, heads, PAIR)[:, :, ::-1]
    sums_two = sum(x[5] for x in down)
    sums_up = sum(x[6] for x in down)
    sums_one = sum(x[4] for x in first)
    small = jnp.concatenate(
        [
            g_rel_table.reshape(-1),
            g_space.reshape(-1),
            sums_one[0],
            sums_two[0],
            sums_one[1],
            sums_two[1],
            sums_up[0],
            sums_two[2],
        ]
    ).reshape(-1, PAIR)
    small = links.sum_all(small).reshape(-1)
    cuts, at = [], 0
    for shape in ((heads, NREL), (2, heads, PAIR), (2, d), (2, d), (ff,), (d,)):
        size = 1
        for s in shape:
            size *= s
        cuts.append(small[at : at + size].reshape(shape))
        at += size
    return (
        result,
        grad_hidden,
        grad_spatial,
        grad_visual,
        g_w_text,
        g_w_vis,
        g_w_out,
        cuts[0],
        cuts[1],
        cuts[2],
        cuts[3],
        g_w_up,
        cuts[4],
        g_w_down,
        cuts[5],
    )


def solution(mesh):
    return jax.shard_map(
        partial(on_device, Links(dict(mesh.shape))),
        mesh=mesh,
        in_specs=(
            P("dp", None),
            P("dp", None),
            P("dp", None),
            P("dp"),
            P("dp"),
            P("dp"),
            P(None, None, "tensor"),
            P(None, None, "tensor"),
            P(None, "tensor", None),
            P("tensor", None),
            P(None, "tensor", None),
            P(),
            P(),
            P(None, "tensor"),
            P("tensor"),
            P("tensor", None),
            P(),
            P("dp", None),
        ),
        out_specs=(
            P("dp", None),
            P("dp", None),
            P("dp", None),
            P("dp", None),
            P(None, "dp", "tensor"),
            P(None, "dp", "tensor"),
            P(None, "tensor", "dp"),
            P("tensor", None),
            P(None, "tensor", None),
            P(),
            P(),
            P("dp", "tensor"),
            P("tensor"),
            P("tensor", "dp"),
            P(),
        ),
        check_vma=False,
    )
```

time: 3160 us -> 457 us (0.14)
  other arithmetic: 1690 us -> 32 us
  local copies, waits for them, and re-layouts: 1100 us -> 103 us
  matrix products: 120 us -> 0 us
  Pallas kernels: 0 us -> 96.6 us
  blocking collectives: 62.7 us -> 0 us
  starting transfers between devices: 0.76 us -> 33.2 us
    scatter-add x3 -> x0, other arithmetic: 1660 us -> none  [the longest x1 1610 us: text_bias(): jnp.take(rel_table, rel_index, axis=1)]
    gather x6, local copies, waits for them, and re-layouts: 973 us -> 14.6 us  [relative_rows(): jnp.take(chunks, self.order(), axis=0, mode='clip').reshape(d, x.shape[0])]
    ppermute x0 -> x38, waiting for transfers between devices: none -> 182 us  [the longest x9 82.1 us: across(): return lax.ppermute(x, 'tensor', [(0, 1), (1, 0)])]
    psum x4 -> x0, waiting for transfers between devices: 156 us -> none  [the longest x1 52.9 us: page_pass(): attention = lax.psum(mixed_product('se,ed->sd', merged, out_flat), 'tensor')]
    dot_general x44 -> x0, matrix products: 120 us -> none  [the longest x36 99.6 us: mixed_product(): jnp.einsum(pattern, left_side, right_side, preferred_element_type=jnp.flo...]
    pallas_call x0 -> x16, Pallas kernels: none -> 96.6 us  [call(): pl.pallas_call(body, out_shape=outs, grid_spec=pltpu.PrefetchScalarGridSp...]
    psum x1 -> x0, blocking collectives: 62.7 us -> none  [on_device(): small_final = lax.psum(small_total, 'dp')]
    convert_element_type x1 -> x0, local copies, waits for them, and re-layouts: 60.6 us -> none  [page_pass(): grad_text_scores.astype(jnp.float32)]
  transfers between devices with their start and end apart: 9 -> 38, of which waited for: 3 -> 17; matrix products, arithmetic and copies ran while one was open for 57% -> 17% of each run, Pallas kernels for 0% -> 18%
where the time goes in v1:
time: 457 us; the launch traced here: 450 us
  waiting for transfers between devices  182 us (40%)
  local copies, waits for them, and re-layouts  103 us (23%)
  Pallas kernels  96.6 us (21%)
  starting transfers between devices  33.2 us (7%)
  other arithmetic  32 us (7%)
    pallas_call x16, Pallas kernels, call(): pl.pallas_call(body, out_shape=outs, grid_spec=pltpu.PrefetchScalarGridSp...  96.6 us
    ppermute x9, waiting for transfers between devices, across(): return lax.ppermute(x, 'tensor', [(0, 1), (1, 0)])  82.1 us
    unnamed x291, local copies, waits for them, and re-layouts  57.2 us
    ppermute x9, waiting for transfers between devices, scatter(): moving = total[turn] + lax.ppermute(moving, 'dp', self.ring)  46.2 us
    ppermute x6, waiting for transfers between devices, scatter(): moving = total[:, turn] + lax.ppermute(moving, 'dp', self.ring)  18.3 us
    ppermute x2, waiting for transfers between devices, scatter(): return moving[0] + lax.ppermute(moving[1], 'dp', self.side)  17.5 us
    ppermute x3, waiting for transfers between devices, scatter(): total = total[0] + lax.ppermute(total[1], 'dp', self.side)  16.4 us
    gather x6, local copies, waits for them, and re-layouts, relative_rows(): jnp.take(chunks, self.order(), axis=0, mode='clip').reshape(d, x.shape[0])  14.6 us
  transfers between devices with their start and end apart: 38, of which 17 were waited for; matrix products, arithmetic and copies ran while one was open for 17% of the time, Pallas kernels for 18%

profile of v1, /device:TPU:0, one launch (start us, length us, event | category | flops | bytes accessed | tf_op | source)
XLA Modules:
  0.0 450.3 jit_solution(10743322582144385744)
XLA Ops:
  12.3 3.8 projections.1
  16.2 13.7 %attention_forward_0.1 = (f32[256,768]{1,0:T(8,128)}, bf16[256,384]{1,0:T(8,128)(2,1)S(1)}, bf16[256,384]{1,0:T(8,128)(2,1)S(1)}, f32[3,256,128]{2,1,0:T(8,128)S(1)}) custom-call(s32[1]{0:T(128)S(6)} %copy.129.vlen, bf16[3,512,256]{2,1,0:T(8,128)(2,1)S(1)} %get-tuple-element.85.tqs, bf16[3,512,128]{2,1,0:T(8,128)(2,1)S(1)} %get-tuple-element.86.vq, ...), custom_call_target="tpu_custom_call" | custom-call | flops 1006632960 | bytes 4000000 | tf_op jit(solution)/shard_map/attention_forward_0/pallas_call | solution.py:37
  32.1 2.9 collective-permute-start
  37.7 13.9 %attention_forward_1.1 = (f32[256,768]{1,0:T(8,128)}, bf16[256,384]{1,0:T(8,128)(2,1)S(1)}, bf16[256,384]{1,0:T(8,128)(2,1)S(1)}, f32[3,256,128]{2,1,0:T(8,128)S(1)}) custom-call(s32[1]{0:T(128)S(6)} %copy.129.vlen, bf16[3,512,256]{2,1,0:T(8,128)(2,1)S(1)} %get-tuple-element.85.tqs, bf16[3,512,128]{2,1,0:T(8,128)(2,1)S(1)} %get-tuple-element.86.vq, ...), custom_call_target="tpu_custom_call" | custom-call | flops 1006632960 | bytes 4000000 | tf_op jit(solution)/shard_map/attention_forward_1/pallas_call | solution.py:37
  57.8 4.9 %feed_forward_0.1 = (f32[256,768]{1,0:T(8,128)S(1)}, f32[256,768]{1,0:T(8,128)S(1)}, bf16[256,768]{1,0:T(8,128)(2,1)S(1)}, bf16[256,1536]{1,0:T(8,128)(2,1)S(1)}...) custom-call(bf16[512,768]{1,0:T(8,128)(2,1)S(1)} %copy-done.4, f32[256,768]{1,0:T(8,128)} %get-tuple-element.91.own, ...), custom_call_target="tpu_custom_call" | custom-call | flops 1207959552 | bytes 9000000 | tf_op jit(solution)/shard_map/feed_forward_0/pallas_call | solution.py:37
  69.2 5.3 %collective-permute-done.2.got = f32[256,768]{1,0:T(8,128)} collective-permute-done((f32[256,768]{1,0:T(8,128)}, f32[256,768]{1,0:T(8,128)}, u32[]{:S(2)}, u32[]{:S(2)}) %collective-permute-start.2) | collective-permute-done | bytes 786464 | tf_op jit(solution)/shard_map/ppermute | solution.py:688
  74.5 4.9 %feed_forward_1.1 = (f32[256,768]{1,0:T(8,128)S(1)}, f32[256,768]{1,0:T(8,128)S(1)}, bf16[256,768]{1,0:T(8,128)(2,1)S(1)}, bf16[256,1536]{1,0:T(8,128)(2,1)S(1)}...) custom-call(bf16[512,768]{1,0:T(8,128)(2,1)S(1)} %copy-done.4, f32[256,768]{1,0:T(8,128)} %get-tuple-element.96.own, ...), custom_call_target="tpu_custom_call" | custom-call | flops 1207959552 | bytes 9000000 | tf_op jit(solution)/shard_map/feed_forward_1/pallas_call | solution.py:37
  92.7 2.8 gather_fusion
  99.1 5.3 %feed_forward_backward_0.1 = (bf16[256,768]{1,0:T(8,128)(2,1)S(1)}, f32[256,768]{1,0:T(8,128)S(1)}, bf16[256,768]{1,0:T(8,128)(2,1)S(1)}, bf16[256,1536]{1,0:T(8...) custom-call(f32[256,768]{1,0:T(8,128)S(1)} %copy-done.47, ...), custom_call_target="tpu_custom_call" | custom-call | flops 1207959552 | bytes 9000000 | tf_op jit(solution)/shard_map/feed_forward_backward_0/pallas_call | solution.py:37
  108.0 5.2 %feed_forward_backward_1.1 = (bf16[256,768]{1,0:T(8,128)(2,1)S(1)}, f32[256,768]{1,0:T(8,128)S(1)}, bf16[256,768]{1,0:T(8,128)(2,1)S(1)}, bf16[256,1536]{1,0:T(8...) custom-call(f32[256,768]{1,0:T(8,128)S(1)} %copy-done.45, ...), custom_call_target="tpu_custom_call" | custom-call | flops 1207959552 | bytes 9000000 | tf_op jit(solution)/shard_map/feed_forward_backward_1/pallas_call | solution.py:37
  121.1 2.8 gather_fusion.4
  128.3 2.7 gather_fusion.5
  132.1 3.2 down_gradient.1
  147.3 10.9 %visual_attention_backward.1 = (bf16[512,384]{1,0:T(8,128)(2,1)S(1)}, bf16[512,768]{1,0:T(8,128)(2,1)S(1)}, f32[512,768]{1,0:T(8,128)S(1)}, f32[3,8,128]{2,1,0:T(8,128)S(1)}) custom-call(s32[1]{0:T(128)S(6)} %copy.129.vlen, bf16[3,512,128]{2,1,0:T(8,128)(2,1)S(1)} %copy-done.23, bf16[3,512,128]{2,1,0:T(8,128)(2,1)S(1)} %copy-done.25, ...), custom_call_target="tpu_custom_call" | custom-call | flops 3623878656 | bytes 5000000 | tf_op jit(solution)/shard_map/visual_attention_backward/pallas_call | solution.py:37
  160.3 15.5 %text_attention_backward.1 = (bf16[512,1152]{1,0:T(8,128)(2,1)S(1)}, bf16[512,768]{1,0:T(8,128)(2,1)S(1)}, f32[512,768]{1,0:T(8,128)S(1)}, f32[512,768]{1,0:T(8,...) custom-call(bf16[3,512,256]{2,1,0:T(8,128)(2,1)S(1)} %copy-done.11, bf16[3,512,256]{2,1,0:T(8,128)(2,1)S(1)} %copy-done.13, ...), custom_call_target="tpu_custom_call" | custom-call | flops 5234491392 | bytes 9000000 | tf_op jit(solution)/shard_map/text_attention_backward/pallas_call | solution.py:37
  183.3 2.9 gather_fusion.3
  193.7 2.9 up_gradient.1
  204.8 4.1 text_projection_gradients.1
  224.9 3.5 collective-permute-done.15
  231.6 2.8 add.649
  240.5 5.2 %collective-permute-done.21 = f32[2,48,768]{2,1,0:T(8,128)S(1)} collective-permute-done((f32[2,48,768]{2,1,0:T(8,128)S(1)}, f32[2,48,768]{2,1,0:T(8,128)S(1)}, u32[]{:S(2)}, u32[]{:S(2)}) %collective-permute-start.21) | collective-permute-done | bytes 294944 | tf_op jit(solution)/shard_map/ppermute | solution.py:704
  245.8 47.9 %collective-permute-done.6 = f32[512,768]{1,0:T(8,128)S(1)} collective-permute-done((f32[512,768]{1,0:T(8,128)}, f32[512,768]{1,0:T(8,128)S(1)}, u32[]{:S(2)}, u32[]{:S(2)}) %collective-permute-start.6) | collective-permute-done | bytes 1572896 | tf_op jit(solution)/shard_map/ppermute | solution.py:688
  296.7 29.0 %collective-permute-done.7 = f32[512,768]{1,0:T(8,128)S(1)} collective-permute-done((f32[512,768]{1,0:T(8,128)S(1)}, f32[512,768]{1,0:T(8,128)S(1)}, u32[]{:S(2)}, u32[]{:S(2)}) %collective-permute-start.7) | collective-permute-done | bytes 1572896 | tf_op jit(solution)/shard_map/ppermute | solution.py:688
  329.3 7.2 %collective-permute-done.17 = f32[2,48,768]{2,1,0:T(8,128)S(1)} collective-permute-done((f32[2,48,768]{2,1,0:T(8,128)S(1)}, f32[2,48,768]{2,1,0:T(8,128)S(1)}, u32[]{:S(2)}, u32[]{:S(2)}) %collective-permute-start.17) | collective-permute-done | bytes 294944 | tf_op jit(solution)/shard_map/ppermute | solution.py:704
  339.4 17.5 %collective-permute-done.23 = f32[48,768]{1,0:T(8,128)S(1)} collective-permute-done((f32[48,768]{1,0:T(8,128)S(1)}, f32[48,768]{1,0:T(8,128)S(1)}, u32[]{:S(2)}, u32[]{:S(2)}) %collective-permute-start.23) | collective-permute-done | bytes 147488 | tf_op jit(solution)/shard_map/ppermute | solution.py:705
  376.2 4.8 %collective-permute-done.35 = f32[48,1536]{1,0:T(8,128)S(1)} collective-permute-done((f32[48,1536]{1,0:T(8,128)S(1)}, f32[48,1536]{1,0:T(8,128)S(1)}, u32[]{:S(2)}, u32[]{:S(2)}) %collective-permute-start.35) | collective-permute-done | bytes 294944 | tf_op jit(solution)/shard_map/ppermute | solution.py:700
  381.1 6.2 %collective-permute-done.30 = f32[48,1536]{1,0:T(8,128)S(1)} collective-permute-done((f32[48,1536]{1,0:T(8,128)S(1)}, f32[48,1536]{1,0:T(8,128)S(1)}, u32[]{:S(2)}, u32[]{:S(2)}) %collective-permute-start.30) | collective-permute-done | bytes 294944 | tf_op jit(solution)/shard_map/ppermute | solution.py:700
  387.4 6.2 %collective-permute-done.36 = f32[48,1536]{1,0:T(8,128)S(1)} collective-permute-done((f32[48,1536]{1,0:T(8,128)S(1)}, f32[48,1536]{1,0:T(8,128)S(1)}, u32[]{:S(2)}, u32[]{:S(2)}) %collective-permute-start.36) | collective-permute-done | bytes 294944 | tf_op jit(solution)/shard_map/ppermute | solution.py:700
  393.7 16.4 %collective-permute-done.10 = f32[4,48,2304]{2,1,0:T(8,128)S(1)} collective-permute-done((f32[4,48,2304]{2,1,0:T(8,128)S(1)}, f32[4,48,2304]{2,1,0:T(8,128)S(1)}, u32[]{:S(2)}, u32[]{:S(2)}) %collective-permute-start.10) | collective-permute-done | bytes 1769504 | tf_op jit(solution)/shard_map/ppermute | solution.py:697
  414.4 10.9 %collective-permute-done.11 = f32[48,2304]{1,0:T(8,128)S(1)} collective-permute-done((f32[48,2304]{1,0:T(8,128)S(1)}, f32[48,2304]{1,0:T(8,128)S(1)}, u32[]{:S(2)}, u32[]{:S(2)}) %collective-permute-start.11) | collective-permute-done | bytes 442400 | tf_op jit(solution)/shard_map/ppermute | solution.py:700
  426.8 10.4 %collective-permute-done.12 = f32[48,2304]{1,0:T(8,128)S(1)} collective-permute-done((f32[48,2304]{1,0:T(8,128)S(1)}, f32[48,2304]{1,0:T(8,128)S(1)}, u32[]{:S(2)}, u32[]{:S(2)}) %collective-permute-start.12) | collective-permute-done | bytes 442400 | tf_op jit(solution)/shard_map/ppermute | solution.py:700
  439.7 7.7 %collective-permute-done.13 = f32[48,2304]{1,0:T(8,128)S(1)} collective-permute-done((f32[48,2304]{1,0:T(8,128)S(1)}, f32[48,2304]{1,0:T(8,128)S(1)}, u32[]{:S(2)}, u32[]{:S(2)}) %collective-permute-start.13) | collective-permute-done | bytes 442400 | tf_op jit(solution)/shard_map/ppermute | solution.py:700
  (474 shorter events, 163.8 us)
Async XLA Ops:
  32.1 23.9 %collective-permute-start = (f32[256,768]{1,0:T(8,128)}, f32[256,768]{1,0:T(8,128)}, u32[]{:S(2)}, u32[]{:S(2)}) collective-permute-start(f32[256,768]{1,0:T(8,128)} %get-tuple-element.91.own), channel_id=1, source_target_pairs={{0,1},{1,0},{2,3},{3,2},{4,5},{5,4},{6,7},{7,6},{8,9},{9,8},{10,11... | collective-permute-start | bytes 2359304 | tf_op jit(solution)/shard_map/ppermute | solution.py:688
  53.7 20.8 %collective-permute-start.2 = (f32[256,768]{1,0:T(8,128)}, f32[256,768]{1,0:T(8,128)}, u32[]{:S(2)}, u32[]{:S(2)}) collective-permute-start(f32[256,768]{1,0:T(8,128)} %get-tuple-element.96.own), channel_id=1, source_target_pairs={{0,1},{1,0},{2,3},{3,2},{4,5},{5,4},{6,7},{7,6},{8,9},{9,8},{10,11... | collective-permute-start | bytes 2359304 | tf_op jit(solution)/shard_map/ppermute | solution.py:688
  67.3 29.8 %collective-permute-start.1 = (f32[256,768]{1,0:T(8,128)}, f32[256,768]{1,0:T(8,128)}, u32[]{:S(2)}, u32[]{:S(2)}) collective-permute-start(f32[256,768]{1,0:T(8,128)} %get-tuple-element.93.own), channel_id=1, source_target_pairs={{0,1},{1,0},{2,3},{3,2},{4,5},{5,4},{6,7},{7,6},{8,9},{9,8},{10,11... | collective-permute-start | bytes 2359304 | tf_op jit(solution)/shard_map/ppermute | solution.py:688
  84.0 23.9 %collective-permute-start.3 = (f32[256,768]{1,0:T(8,128)}, f32[256,768]{1,0:T(8,128)}, u32[]{:S(2)}, u32[]{:S(2)}) collective-permute-start(f32[256,768]{1,0:T(8,128)} %get-tuple-element.98.own), channel_id=1, source_target_pairs={{0,1},{1,0},{2,3},{3,2},{4,5},{5,4},{6,7},{7,6},{8,9},{9,8},{10,11... | collective-permute-start | bytes 2359304 | tf_op jit(solution)/shard_map/ppermute | solution.py:688
  106.0 31.7 %collective-permute-start.4 = (f32[256,768]{1,0:T(8,128)}, f32[256,768]{1,0:T(8,128)}, u32[]{:S(2)}, u32[]{:S(2)}) collective-permute-start(f32[256,768]{1,0:T(8,128)} %get-tuple-element.102.own), channel_id=1, source_target_pairs={{0,1},{1,0},{2,3},{3,2},{4,5},{5,4},{6,7},{7,6},{8,9},{9,8},{10,11... | collective-permute-start | bytes 2359304 | tf_op jit(solution)/shard_map/ppermute | solution.py:688
  117.7 25.3 %collective-permute-start.5 = (f32[256,768]{1,0:T(8,128)}, f32[256,768]{1,0:T(8,128)}, u32[]{:S(2)}, u32[]{:S(2)}) collective-permute-start(f32[256,768]{1,0:T(8,128)} %get-tuple-element.106.own), channel_id=1, source_target_pairs={{0,1},{1,0},{2,3},{3,2},{4,5},{5,4},{6,7},{7,6},{8,9},{9,8},{10,11... | collective-permute-start | bytes 2359304 | tf_op jit(solution)/shard_map/ppermute | solution.py:688
  135.3 95.5 %collective-permute-start.33 = (f32[384,1536]{1,0:T(8,128)}, f32[384,1536]{1,0:T(8,128)}, u32[]{:S(2)}, u32[]{:S(2)}) collective-permute-start(f32[384,1536]{1,0:T(8,128)} %get-tuple-element.154), channel_id=1, source_target_pairs={{0,2},{2,0},{4,6},{6,4},{8,10},{10,8},{12,14},{14,12},{16,18},{18,... | collective-permute-start | bytes 7077896 | tf_op jit(solution)/shard_map/ppermute | solution.py:695
  188.7 20.8 %collective-permute-start.19 = (f32[384,768]{1,0:T(8,128)S(1)}, f32[384,768]{1,0:T(8,128)S(1)}, u32[]{:S(2)}, u32[]{:S(2)}) collective-permute-start(f32[384,768]{1,0:T(8,128)S(1)} %get-tuple-element.133), channel_id=1, source_target_pairs={{0,2},{2,0},{4,6},{6,4},{8,10},{10,8},{12,14},{14,12},{16,18},{18,... | collective-permute-start | bytes 3538952 | tf_op jit(solution)/shard_map/ppermute | solution.py:695
  191.2 20.9 %collective-permute-start.14 = (f32[384,768]{1,0:T(8,128)S(1)}, f32[384,768]{1,0:T(8,128)S(1)}, u32[]{:S(2)}, u32[]{:S(2)}) collective-permute-start(f32[384,768]{1,0:T(8,128)S(1)} %get-tuple-element.125), channel_id=1, source_target_pairs={{0,2},{2,0},{4,6},{6,4},{8,10},{10,8},{12,14},{14,12},{16,18},{18,... | collective-permute-start | bytes 3538952 | tf_op jit(solution)/shard_map/ppermute | solution.py:695
  198.1 37.8 %collective-permute-start.28 = (f32[384,1536]{1,0:T(8,128)}, f32[384,1536]{1,0:T(8,128)}, u32[]{:S(2)}, u32[]{:S(2)}) collective-permute-start(f32[384,1536]{1,0:T(8,128)} %get-tuple-element.148), channel_id=1, source_target_pairs={{0,2},{2,0},{4,6},{6,4},{8,10},{10,8},{12,14},{14,12},{16,18},{18,... | collective-permute-start | bytes 7077896 | tf_op jit(solution)/shard_map/ppermute | solution.py:695
  208.9 162.0 %collective-permute-start.9 = (f32[384,2304]{1,0:T(8,128)}, f32[384,2304]{1,0:T(8,128)}, u32[]{:S(2)}, u32[]{:S(2)}) collective-permute-start(f32[384,2304]{1,0:T(8,128)} %get-tuple-element.122), channel_id=1, source_target_pairs={{0,2},{2,0},{4,6},{6,4},{8,10},{10,8},{12,14},{14,12},{16,18},{18,... | collective-permute-start | bytes 10616840 | tf_op jit(solution)/shard_map/ppermute | solution.py:695
  210.5 11.9 %collective-permute-start.20 = (f32[2,48,768]{2,1,0:T(8,128)}, f32[2,48,768]{2,1,0:T(8,128)}, u32[]{:S(2)}, u32[]{:S(2)}) collective-permute-start(f32[2,48,768]{2,1,0:T(8,128)} %slice_bitcast_fusion.12), channel_id=1, source_target_pairs={{0,8},{2,10},{4,12},{6,14},{8,16},{10,18},{12,20},{14,22},{16,24},... | collective-permute-start | bytes 884744 | tf_op jit(solution)/shard_map/ppermute | solution.py:704
  214.1 14.3 %collective-permute-start.15 = (f32[2,48,768]{2,1,0:T(8,128)}, f32[2,48,768]{2,1,0:T(8,128)}, u32[]{:S(2)}, u32[]{:S(2)}) collective-permute-start(f32[2,48,768]{2,1,0:T(8,128)} %slice_bitcast_fusion.16), channel_id=1, source_target_pairs={{0,8},{2,10},{4,12},{6,14},{8,16},{10,18},{12,20},{14,22},{16,24},... | collective-permute-start | bytes 884744 | tf_op jit(solution)/shard_map/ppermute | solution.py:704
  222.4 72.4 %collective-permute-start.8 = (f32[512,768]{1,0:T(8,128)}, f32[512,768]{1,0:T(8,128)S(1)}, u32[]{:S(2)}, u32[]{:S(2)}) collective-permute-start(f32[512,768]{1,0:T(8,128)} %copy-done.28), channel_id=1, source_target_pairs={{0,1},{1,0},{2,3},{3,2},{4,5},{5,4},{6,7},{7,6},{8,9},{9,8},{10,11... | collective-permute-start | bytes 4718600 | tf_op jit(solution)/shard_map/ppermute | solution.py:688
  228.4 65.3 %collective-permute-start.6 = (f32[512,768]{1,0:T(8,128)}, f32[512,768]{1,0:T(8,128)S(1)}, u32[]{:S(2)}, u32[]{:S(2)}) collective-permute-start(f32[512,768]{1,0:T(8,128)} %copy-done.32), channel_id=1, source_target_pairs={{0,1},{1,0},{2,3},{3,2},{4,5},{5,4},{6,7},{7,6},{8,9},{9,8},{10,11... | collective-permute-start | bytes 4718600 | tf_op jit(solution)/shard_map/ppermute | solution.py:688
  230.9 94.8 %collective-permute-start.7 = (f32[512,768]{1,0:T(8,128)S(1)}, f32[512,768]{1,0:T(8,128)S(1)}, u32[]{:S(2)}, u32[]{:S(2)}) collective-permute-start(f32[512,768]{1,0:T(8,128)S(1)} %copy-done.31), channel_id=1, source_target_pairs={{0,1},{1,0},{2,3},{3,2},{4,5},{5,4},{6,7},{7,6},{8,9},{9,8},{10,11... | collective-permute-start | bytes 4718600 | tf_op jit(solution)/shard_map/ppermute | solution.py:688
  245.7 81.8 %collective-permute-start.16 = (f32[2,48,768]{2,1,0:T(8,128)S(1)}, f32[2,48,768]{2,1,0:T(8,128)S(1)}, u32[]{:S(2)}, u32[]{:S(2)}) collective-permute-start(f32[2,48,768]{2,1,0:T(8,128)S(1)} %fusion.14), channel_id=1, source_target_pairs={{0,8},{2,10},{4,12},{6,14},{8,16},{10,18},{12,20},{14,22},{16,24},... | collective-permute-start | bytes 884744 | tf_op jit(solution)/shard_map/ppermute | solution.py:704
  293.7 34.0 %collective-permute-start.22 = (f32[2,48,768]{2,1,0:T(8,128)S(1)}, f32[2,48,768]{2,1,0:T(8,128)S(1)}, u32[]{:S(2)}, u32[]{:S(2)}) collective-permute-start(f32[2,48,768]{2,1,0:T(8,128)S(1)} %fusion.12), channel_id=1, source_target_pairs={{0,8},{2,10},{4,12},{6,14},{8,16},{10,18},{12,20},{14,22},{16,24},... | collective-permute-start | bytes 884744 | tf_op jit(solution)/shard_map/ppermute | solution.py:704
  294.8 72.6 %collective-permute-start.34 = (f32[4,48,1536]{2,1,0:T(8,128)}, f32[4,48,1536]{2,1,0:T(8,128)}, u32[]{:S(2)}, u32[]{:S(2)}) collective-permute-start(f32[4,48,1536]{2,1,0:T(8,128)} %bitcast.74), channel_id=1, source_target_pairs={{0,4},{2,6},{4,0},{6,2},{8,12},{10,14},{12,8},{14,10},{16,20},{18,... | collective-permute-start | bytes 3538952 | tf_op jit(solution)/shard_map/ppermute | solution.py:697
  325.7 43.7 %collective-permute-start.29 = (f32[4,48,1536]{2,1,0:T(8,128)}, f32[4,48,1536]{2,1,0:T(8,128)}, u32[]{:S(2)}, u32[]{:S(2)}) collective-permute-start(f32[4,48,1536]{2,1,0:T(8,128)} %bitcast.64), channel_id=1, source_target_pairs={{0,4},{2,6},{4,0},{6,2},{8,12},{10,14},{12,8},{14,10},{16,20},{18,... | collective-permute-start | bytes 3538952 | tf_op jit(solution)/shard_map/ppermute | solution.py:697
  327.7 29.2 %collective-permute-start.23 = (f32[48,768]{1,0:T(8,128)S(1)}, f32[48,768]{1,0:T(8,128)S(1)}, u32[]{:S(2)}, u32[]{:S(2)}) collective-permute-start(f32[48,768]{1,0:T(8,128)S(1)} %slice_bitcast_fusion.20), channel_id=1, source_target_pairs={{0,4},{2,6},{4,0},{6,2},{8,12},{10,14},{12,8},{14,10},{16,20},{18,... | collective-permute-start | bytes 442376 | tf_op jit(solution)/shard_map/ppermute | solution.py:705
  337.9 23.0 %collective-permute-start.18 = (f32[48,768]{1,0:T(8,128)}, f32[48,768]{1,0:T(8,128)}, u32[]{:S(2)}, u32[]{:S(2)}) collective-permute-start(f32[48,768]{1,0:T(8,128)} %slice_bitcast_fusion.22), channel_id=1, source_target_pairs={{0,4},{2,6},{4,0},{6,2},{8,12},{10,14},{12,8},{14,10},{16,20},{18,... | collective-permute-start | bytes 442376 | tf_op jit(solution)/shard_map/ppermute | solution.py:705
  369.3 11.6 %collective-permute-start.35 = (f32[48,1536]{1,0:T(8,128)S(1)}, f32[48,1536]{1,0:T(8,128)S(1)}, u32[]{:S(2)}, u32[]{:S(2)}) collective-permute-start(f32[48,1536]{1,0:T(8,128)S(1)} %slice_bitcast_fusion.4), channel_id=1, source_target_pairs={{0,8},{2,10},{4,12},{6,14},{8,16},{10,18},{12,20},{14,22},{16,24},... | collective-permute-start | bytes 884744 | tf_op jit(solution)/shard_map/ppermute | solution.py:700
  373.5 36.6 %collective-permute-start.10 = (f32[4,48,2304]{2,1,0:T(8,128)S(1)}, f32[4,48,2304]{2,1,0:T(8,128)S(1)}, u32[]{:S(2)}, u32[]{:S(2)}) collective-permute-start(f32[4,48,2304]{2,1,0:T(8,128)S(1)} %bitcast.208), channel_id=1, source_target_pairs={{0,4},{2,6},{4,0},{6,2},{8,12},{10,14},{12,8},{14,10},{16,20},{18,... | collective-permute-start | bytes 5308424 | tf_op jit(solution)/shard_map/ppermute | solution.py:697
  374.1 13.2 %collective-permute-start.30 = (f32[48,1536]{1,0:T(8,128)S(1)}, f32[48,1536]{1,0:T(8,128)S(1)}, u32[]{:S(2)}, u32[]{:S(2)}) collective-permute-start(f32[48,1536]{1,0:T(8,128)S(1)} %slice_bitcast_fusion.8), channel_id=1, source_target_pairs={{0,8},{2,10},{4,12},{6,14},{8,16},{10,18},{12,20},{14,22},{16,24},... | collective-permute-start | bytes 884744 | tf_op jit(solution)/shard_map/ppermute | solution.py:700
  381.0 12.6 %collective-permute-start.36 = (f32[48,1536]{1,0:T(8,128)S(1)}, f32[48,1536]{1,0:T(8,128)S(1)}, u32[]{:S(2)}, u32[]{:S(2)}) collective-permute-start(f32[48,1536]{1,0:T(8,128)S(1)} %fusion.4), channel_id=1, source_target_pairs={{0,8},{2,10},{4,12},{6,14},{8,16},{10,18},{12,20},{14,22},{16,24},... | collective-permute-start | bytes 884744 | tf_op jit(solution)/shard_map/ppermute | solution.py:700
  387.3 25.4 %collective-permute-start.31 = (f32[48,1536]{1,0:T(8,128)S(1)}, f32[48,1536]{1,0:T(8,128)S(1)}, u32[]{:S(2)}, u32[]{:S(2)}) collective-permute-start(f32[48,1536]{1,0:T(8,128)S(1)} %fusion.8), channel_id=1, source_target_pairs={{0,8},{2,10},{4,12},{6,14},{8,16},{10,18},{12,20},{14,22},{16,24},... | collective-permute-start | bytes 884744 | tf_op jit(solution)/shard_map/ppermute | solution.py:700
  393.7 32.3 %collective-permute-start.37 = (f32[48,1536]{1,0:T(8,128)S(1)}, f32[48,1536]{1,0:T(8,128)S(1)}, u32[]{:S(2)}, u32[]{:S(2)}) collective-permute-start(f32[48,1536]{1,0:T(8,128)S(1)} %fusion.5), channel_id=1, source_target_pairs={{0,8},{2,10},{4,12},{6,14},{8,16},{10,18},{12,20},{14,22},{16,24},... | collective-permute-start | bytes 884744 | tf_op jit(solution)/shard_map/ppermute | solution.py:700
  410.4 15.0 %collective-permute-start.11 = (f32[48,2304]{1,0:T(8,128)S(1)}, f32[48,2304]{1,0:T(8,128)S(1)}, u32[]{:S(2)}, u32[]{:S(2)}) collective-permute-start(f32[48,2304]{1,0:T(8,128)S(1)} %slice_bitcast_fusion), channel_id=1, source_target_pairs={{0,8},{2,10},{4,12},{6,14},{8,16},{10,18},{12,20},{14,22},{16,24},... | collective-permute-start | bytes 1327112 | tf_op jit(solution)/shard_map/ppermute | solution.py:700
  412.8 26.1 %collective-permute-start.32 = (f32[48,1536]{1,0:T(8,128)S(1)}, f32[48,1536]{1,0:T(8,128)S(1)}, u32[]{:S(2)}, u32[]{:S(2)}) collective-permute-start(f32[48,1536]{1,0:T(8,128)S(1)} %fusion.9), channel_id=1, source_target_pairs={{0,8},{2,10},{4,12},{6,14},{8,16},{10,18},{12,20},{14,22},{16,24},... | collective-permute-start | bytes 884744 | tf_op jit(solution)/shard_map/ppermute | solution.py:700
  425.4 11.7 %collective-permute-start.12 = (f32[48,2304]{1,0:T(8,128)S(1)}, f32[48,2304]{1,0:T(8,128)S(1)}, u32[]{:S(2)}, u32[]{:S(2)}) collective-permute-start(f32[48,2304]{1,0:T(8,128)S(1)} %fusion.1), channel_id=1, source_target_pairs={{0,8},{2,10},{4,12},{6,14},{8,16},{10,18},{12,20},{14,22},{16,24},... | collective-permute-start | bytes 1327112 | tf_op jit(solution)/shard_map/ppermute | solution.py:700
  437.2 10.2 %collective-permute-start.13 = (f32[48,2304]{1,0:T(8,128)S(1)}, f32[48,2304]{1,0:T(8,128)S(1)}, u32[]{:S(2)}, u32[]{:S(2)}) collective-permute-start(f32[48,2304]{1,0:T(8,128)S(1)} %fusion.2), channel_id=1, source_target_pairs={{0,8},{2,10},{4,12},{6,14},{8,16},{10,18},{12,20},{14,22},{16,24},... | collective-permute-start | bytes 1327112 | tf_op jit(solution)/shard_map/ppermute | solution.py:700
  (144 other events, 891.8 us)
